TPU v7x, 768 devices: a whole 4x8x12 slice. The times are simulated.
768 devices in a mesh: dp: 96 (over y, z), shard: 8 (over x, core).
Axes of the slice: x: 4, y: 8, z: 12, core: 2. Of those that a mesh axis runs over, the one named last changes fastest.
Arguments:
- grad_partials: bfloat16 [96, 8, 1536, 512], P('dp', 'shard')
Outputs:
- update_blocks: float32 [8, 1536, 512], P('shard', 'dp')
All inputs are finite; a program needn't handle non-finite values.
Results may differ from a plain program's by a relative error of at most 0.0059.
Values may be sent and summed in bfloat16 or wider, within the bound.
A program may use at most 32 MiB of HBM per device.

v0:
```python
import math

import jax
import jax.numpy as jnp
from jax import lax
from jax.sharding import PartitionSpec as P

ITERS = 2


ridge = 0.1
target_rms = 0.5


def spread(block, axis, holder):
    block = jnp.where(lax.axis_index(axis) == holder, block, jnp.zeros_like(block))
    return lax.psum(block, axis)


def matmul_high(left, right):
    return jnp.dot(left, right, precision=lax.Precision.HIGHEST, preferred_element_type=jnp.float32)


def newton_root(statistic):
    identity = jnp.eye(statistic.shape[0], dtype=jnp.float32)
    norm_scale = jnp.sqrt(jnp.sum(statistic * statistic))
    moment = statistic / norm_scale
    start_scale = norm_scale ** (-0.25)
    iterate = identity * start_scale
    for iteration in range(ITERS):
        factor = (5.0 * identity - moment) * 0.25
        if iteration == 0:
            iterate = factor * start_scale
        else:
            iterate = matmul_high(iterate, factor)
        if iteration + 1 < ITERS:
            square = matmul_high(factor, factor)
            fourth = matmul_high(square, square)
            moment = matmul_high(fourth, moment)
    return iterate.astype(jnp.bfloat16)


def spare_root(statistic):
    return jnp.zeros(statistic.shape, jnp.bfloat16)


def left_statistic(block, identity, width):
    return (
        jnp.einsum("ab,cb->ac", block, block, preferred_element_type=jnp.float32) / width
        + ridge * identity
    )


def body(grad_partials):
    dp_count = lax.axis_size("dp")
    shard_count = lax.axis_size("shard")
    local_term = grad_partials[0, 0].astype(jnp.float32)
    width = local_term.shape[1]
    block_count = local_term.shape[0] // width
    limit = target_rms * width * math.sqrt(block_count * shard_count)
    identity = jnp.eye(width, dtype=jnp.float32)
    band_sum = lax.psum_scatter(local_term, "dp", scatter_dimension=0, tiled=True)
    sumsq = lax.psum(jnp.sum(band_sum * band_sum), ("dp", "shard"))
    clip_factor = limit / jnp.sqrt(sumsq)
    column = lax.all_gather((band_sum * clip_factor).astype(jnp.bfloat16), "dp", axis=0, tiled=True)
    blocks = column.reshape(block_count, width, width)
    dp_index = lax.axis_index("dp")
    band_rows = block_count * width // dp_count
    row_start = dp_index * band_rows
    first_block = row_start // width
    global_rows = row_start + jnp.arange(band_rows, dtype=jnp.int32)
    touched_ids = [jnp.minimum(first_block + 0, block_count - 1)]
    touched_blocks = [
        lax.dynamic_index_in_dim(blocks, block_id, 0, keepdims=False) for block_id in touched_ids
    ]
    side_total = 2 * block_count
    side_id = dp_index + 0
    has_side = side_id < side_total
    block_index = jnp.minimum(side_id // 2, block_count - 1)
    side_flag = side_id % 2
    block = lax.dynamic_index_in_dim(blocks, block_index, 0, keepdims=False)
    chosen = jnp.where(side_flag == 0, block, block.T)
    statistic = left_statistic(chosen, identity, width)
    owned = [lax.cond(has_side, newton_root, spare_root, statistic)]
    shared = []
    for side_index in range(side_total):
        shared.append(spread(owned[side_index // dp_count], "dp", side_index % dp_count))
    left_roots = jnp.stack(shared[0::2])
    right_roots = jnp.stack(shared[1::2])
    left_picks = [
        lax.dynamic_index_in_dim(left_roots, block_id, 0, keepdims=False)
        for block_id in touched_ids
    ]
    right_picks = [
        lax.dynamic_index_in_dim(right_roots, block_id, 0, keepdims=False)
        for block_id in touched_ids
    ]
    hidden_acc = jnp.zeros((band_rows, width), jnp.float32)
    offset = 0
    inside = global_rows // width == first_block + offset
    inside_masks = [inside]
    local_rows = jnp.clip(global_rows - touched_ids[offset] * width, 0, width - 1)
    left_rows = jnp.take(left_picks[offset], local_rows, axis=0)
    product = jnp.dot(left_rows, touched_blocks[offset], preferred_element_type=jnp.float32)
    hidden_acc = jnp.where(inside[:, None], product, hidden_acc)
    hidden = hidden_acc.astype(jnp.bfloat16)
    update_band = jnp.zeros((band_rows, width), jnp.float32)
    offset = 0
    product = jnp.dot(hidden, right_picks[offset], preferred_element_type=jnp.float32)
    update_band = jnp.where(inside_masks[offset][:, None], product, update_band)
    return update_band[None]


def solution(mesh):
    placed = (P("dp", "shard", None, None),)
    return jax.shard_map(
        body, mesh=mesh, in_specs=placed, out_specs=P("shard", "dp", None), check_vma=False
    )
```

profile of v0, /device:TPU:4, one launch (start us, length us, event | category | flops | bytes accessed | tf_op | source)
XLA Modules:
  0.0 1201.2 jit_solution(10173675336163875311)
XLA Ops:
  6.5 0.0 reduce-scatter.2.cloned.1.call-start
  6.5 3.5 bitcast_convert_fusion
  10.0 0.0 reduce-scatter.2.cloned.1.call-update
  10.1 0.0 all-gather.2.cloned.1.call-start
  10.1 690.3 %reduce-scatter.2.cloned.1.call-done = f32[16,512]{1,0:T(8,128)} async-done(((f32[1536,512]{1,0:T(8,128)}), f32[16,512]{1,0:T(8,128)}) %reduce-scatter.2.cloned.1.call-update) | async-done | bytes 32784 | tf_op jit(solution)/shard_map/reduce_scatter | solution.py:62
  700.4 1.4 multiply_reduce_fusion.1
  701.8 105.6 %psum.49 = f32[]{:T(128)} all-reduce(f32[]{:T(128)} %multiply_reduce_fusion.1), channel_id=1, replica_groups=mesh['dp'=96,'shard'=8] {'dp','shard'}, use_global_device_ids=true, to_apply=%region_2.0 | all-reduce | flops 1 | bytes 8 | tf_op jit(solution)/shard_map/psum | solution.py:63
  808.1 1.4 multiply_convert_fusion
  809.5 0.0 all-gather.2.cloned.1.call-update
  809.5 0.0 all-reduce.3.cloned.1.call-start
  809.6 118.6 %all-gather.2.cloned.1.call-done = bf16[1536,512]{1,0:T(8,128)(2,1)} async-done(((bf16[16,512]{1,0:T(8,128)(2,1)}), bf16[1536,512]{1,0:T(8,128)(2,1)}) %all-gather.2.cloned.1.call-update) | async-done | bytes 1572880 | tf_op jit(solution)/shard_map/all_gather | solution.py:65
  928.1 1.1 dynamic-slice_bitcast_fusion
  929.2 0.2 copy.3
  929.4 0.5 fusion.26
  929.9 0.1 iota.35
  930.0 0.1 iota.36
  930.1 9.5 conditional.1
  930.1 1.1 multiply_reduce_fusion
  931.9 2.0 fusion.1
  933.9 1.8 fusion.46
  935.7 1.9 fusion
  937.7 2.0 convolution_convert_fusion
  939.6 1.7 select_bitcast_fusion.3
  941.3 0.0 all-reduce.3.cloned.1.call-update
  941.4 249.0 %all-reduce.3.cloned.1.call-done = (bf16[1,512,512]{2,1,0:T(8,128)(2,1)}, bf16[1,512,512]{2,1,0:T(8,128)(2,1)}, bf16[1,512,512]{2,1,0:T(8,128)(2,1)}, bf16[1,512...) async-done(((bf16[1,512,512]{2,1,0:T(8,128)(2,1)}, bf16[1,512,512]{2,1,0:T(8,128)(2,1)}, bf16[1,512,512]{2,1,0:T(8,128)(2,1)}, ...) | async-done | bytes 3145744 | tf_op jit(solution)/shard_map/psum | solution.py:17
  1190.4 0.0 copy-start
  1190.4 0.0 copy-start.1
  1190.4 0.0 copy-start.2
  1190.4 1.5 fusion.23
  1191.9 0.6 gather_fusion
  1192.4 0.0 copy-done
  1192.5 0.0 copy-done.1
  1192.5 0.0 copy-done.2
  1192.5 2.2 fusion.15
  (3 shorter events, 0.0 us)
Async XLA Ops:
  6.5 693.9 %reduce-scatter.2.cloned.1.call-start = ((), (), s32[]{:S(2)}) async-start(), calls=%async_computation.1 | async-start | bytes 3178496 | tf_op jit(solution)/shard_map/reduce_scatter | solution.py:62
  10.1 918.1 %all-gather.2.cloned.1.call-start = ((), (), s32[]{:S(2)}) async-start(), calls=%async_computation.2 | async-start | bytes 1589248 | tf_op jit(solution)/shard_map/all_gather | solution.py:65
  809.5 380.9 %all-reduce.3.cloned.1.call-start = ((), (), s32[]{:S(2)}) async-start(), calls=%async_computation.3 | async-start | bytes 6291456 | tf_op jit(solution)/shard_map/psum | solution.py:17
  1190.4 2.1 copy-start
  1190.4 2.1 copy-start.1
  1190.4 2.1 copy-start.2
Sparse Core Ops, SparseCore 0:
  12.5 687.8 reduce-scatter.1
  809.6 118.4 all-gather.1
  941.5 248.8 all-reduce.2
where the time goes:
time: 1200 us
  waiting for transfers between devices  1060 us (88%)
  blocking collectives  106 us (9%)
  between operations  14 us (1%)
    reduce_scatter x1, waiting for transfers between devices, body(): lax.psum_scatter(local_term, 'dp', scatter_dimension=0, tiled=True)  690 us
    psum x1, waiting for transfers between devices, spread(): return lax.psum(block, axis)  249 us
    all_gather x1, waiting for transfers between devices, body(): lax.all_gather((band_sum * clip_factor).astype(jnp.bfloat16), 'dp', axis=...  119 us
    psum x1, blocking collectives, body(): sumsq = lax.psum(jnp.sum(band_sum * band_sum), ('dp', 'shard'))  106 us
  transfers between devices with their start and end apart: 3, of which 3 were waited for; matrix products, arithmetic and copies ran while one was open for 0% of the time, Pallas kernels for 0%

commit v1 on v0

v1 whole, which is shorter than its diff:
```python
import functools
import math

import jax
import jax.numpy as jnp
from jax import lax
from jax.experimental import pallas as pl
from jax.experimental.pallas import tpu as pltpu
from jax.sharding import PartitionSpec as P

MESH = pl.DeviceIdType.MESH
NY, NZ, NS = 8, 12, 8
PARTS = 4
PER_BLOCK = 32
BLOCKS = 3
ROOTS = BLOCKS * NS
RIDGE = 0.1
TARGET_RMS = 0.5
F32, BF16 = jnp.float32, jnp.bfloat16


def series():
    coefs = [25.0 / 16.0, -5.0 / 16.0, 0.0, 0.0, 0.0, 0.0, 0.0]
    for power in range(6):
        coefs[power + 1] -= math.comb(5, power) * 5.0 ** (5 - power) * (-1.0) ** power / 4096.0
    return coefs


def shifted(beta, gamma):
    coefs = series()
    out = []
    scale = jnp.ones_like(beta)
    for j in range(7):
        total = jnp.zeros_like(beta)
        for i in range(6, j - 1, -1):
            total = total * gamma + coefs[i] * math.comb(i, j)
        out.append(total * scale)
        scale = scale * beta
    return out


def root_of(block, shard):
    row = 1 + 2 * block + block // 2
    return row * NZ + lax.rem(shard, 2)


def dot(a, b, dims):
    return lax.dot_general(a, b, (dims, ((), ())), preferred_element_type=F32)


NN = ((1,), (0,))
NT = ((1,), (1,))
TN = ((0,), (0,))


def kernel(
    g_ref, out_ref,
    loc, rbuf, lbuf, rsend, lsend, zsend, own, zbuf, piece, sq, gath, gsq, tot, xbuf, upd, land,
    loc_sem, rs_sem, rr_sem, ls_sem, lr_sem, zs_sem, zr_sem, gs_sem, gr_sem, qs_sem, qr_sem,
    xs_sem, xr_sem, us_sem, ur_sem,
):
    i = lax.axis_index("dp")
    s = lax.axis_index("shard")
    y, z = i // NZ, lax.rem(i, NZ)
    block, mine = i // PER_BLOCK, lax.rem(i, PER_BLOCK)
    root = root_of(block, s)
    is_root = i == root
    here = block * NS + s

    def yy(d):
        return lax.rem(y + d + NY, NY)

    def zz(d):
        return lax.rem(z + d + NZ, NZ)

    def remote(src, dst, ssem, rsem, dev):
        return pltpu.make_async_remote_copy(
            src_ref=src, dst_ref=dst, send_sem=ssem, recv_sem=rsem,
            device_id=dev, device_id_type=MESH,
        )

    local = pltpu.make_async_copy(g_ref, loc, loc_sem)
    local.start()

    barrier = pltpu.get_barrier_semaphore()

    def greet(dp, shard):
        pl.semaphore_signal(barrier, inc=1, device_id=(dp, shard), device_id_type=MESH)

    up, down = yy(1) * NZ + z, yy(-1) * NZ + z
    greet(up, s)
    greet(down, s)
    for d in range(1, NZ):
        greet(y * NZ + zz(d), s)

    @pl.when(is_root)
    def _():
        @pl.loop(1, PER_BLOCK)
        def _(d):
            greet(block * PER_BLOCK + lax.rem(mine + d, PER_BLOCK), s)

        @pl.loop(1, ROOTS)
        def _(d):
            q = lax.rem(here + d, ROOTS)
            greet(root_of(q // NS, lax.rem(q, NS)), lax.rem(q, NS))

        pl.semaphore_wait(barrier, 2 + NZ - 1 + PER_BLOCK - 1 + ROOTS - 1)

    @pl.when(jnp.logical_not(is_root))
    def _():
        greet(root, s)
        pl.semaphore_wait(barrier, 2 + NZ - 1 + 1)

    def count(way, j):
        return 4 if (j < PARTS // 2) == (way > 0) else 3

    tables = {1: (rbuf, rsend, rs_sem, rr_sem), -1: (lbuf, lsend, ls_sem, lr_sem)}
    started = []

    def ring(way, j, t):
        buf, sends, ssem, rsem = tables[way]
        src = g_ref.at[yy(way * count(way, j)), :, j] if t == 0 else sends.at[j, t - 1]
        return remote(src, buf.at[j, t], ssem.at[j, t], rsem.at[j, t], (up if way > 0 else down, s))

    for t in range(4):
        for j in range(PARTS):
            for way in (1, -1):
                if t >= count(way, j):
                    continue
                if t > 0:
                    if t == 1 and j == 0 and way == 1:
                        local.wait()
                    buf, sends, _, _ = tables[way]
                    ring(way, j, t - 1).wait_recv()
                    chunk = yy(way * (count(way, j) - t))
                    sends[j, t - 1] = (
                        loc[chunk, :, j].astype(F32) + buf[j, t - 1].astype(F32)
                    ).astype(BF16)
                copy = ring(way, j, t)
                copy.start()
                started.append(copy)

    def across(j, a):
        to = 4 * a + j
        return to, remote(
            zsend.at[j, a], zbuf.at[lax.rem(to - z + NZ, NZ)], zs_sem.at[to],
            zr_sem.at[lax.rem(to - z + NZ, NZ)], (y * NZ + to, s),
        )

    for j in range(PARTS):
        ring(1, j, count(1, j) - 1).wait_recv()
        ring(-1, j, count(-1, j) - 1).wait_recv()
        total = (
            loc[y, :, j].astype(F32)
            + rbuf[j, count(1, j) - 1].astype(F32)
            + lbuf[j, count(-1, j) - 1].astype(F32)
        )
        zsend[j] = total.astype(BF16)
        for a in range(3):
            to, copy = across(j, a)

            @pl.when(z != to)
            def _():
                copy.start()

            @pl.when(z == to)
            def _():
                own[...] = total[a]

    rows = own[...]
    for d in range(1, NZ):
        remote(zsend.at[0, 0], zbuf.at[d], zs_sem.at[0], zr_sem.at[d], (up, s)).wait_recv()
        rows = rows + zbuf[d].astype(F32)

    piece[...] = rows.astype(BF16)
    squares = rows * rows
    folded = squares[0:8] + squares[8:16]
    sq[...] = folded[:, 0:128] + folded[:, 128:256] + folded[:, 256:384] + folded[:, 384:512]

    def to_root(slot):
        return (
            remote(piece, gath.at[slot], gs_sem, gr_sem.at[slot], (root, s)),
            remote(sq, gsq.at[slot], qs_sem, qr_sem.at[slot], (root, s)),
        )

    @pl.when(jnp.logical_not(is_root))
    def _():
        for copy in to_root(mine):
            copy.start()

    def from_root(m):
        return remote(
            upd.at[m], land, us_sem.at[m], ur_sem, (block * PER_BLOCK + m, s)
        )

    @pl.when(is_root)
    def _():
        gath[mine] = piece[...]
        gsq[mine] = sq[...]

        @pl.loop(1, PER_BLOCK)
        def _(d):
            for copy in to_root(lax.rem(mine + d, PER_BLOCK)):
                copy.wait_recv()

        block_sq = jnp.sum(gsq[...], axis=0)
        tot[...] = block_sq

        def to_other(q, slot):
            return remote(
                tot, xbuf.at[slot], xs_sem.at[q], xr_sem.at[slot],
                (root_of(q // NS, lax.rem(q, NS)), lax.rem(q, NS)),
            )

        @pl.loop(1, ROOTS)
        def _(d):
            to_other(lax.rem(here + d, ROOTS), here).start()

        width = 16 * PER_BLOCK
        grad = gath[...].reshape(width, width)
        fb = jnp.sum(block_sq, keepdims=True)
        inverse = jnp.where(fb > 0.0, 1.0 / fb, 0.0)
        left = dot(grad, grad, NT) * inverse
        right = dot(grad, grad, TN) * inverse
        eye = lax.broadcasted_iota(jnp.int32, (width, width), 0) == lax.broadcasted_iota(
            jnp.int32, (width, width), 1
        )
        trace = jnp.sum(jnp.where(eye, left, 0.0), keepdims=True)
        norm2 = jnp.sum(left * left, keepdims=True)

        def powers(n):
            nb = n.astype(BF16)
            q = dot(nb, nb, NN)
            return q, dot(nb, q.astype(BF16), NN)

        left2, left3 = powers(left)
        right2, right3 = powers(right)

        xbuf[here] = block_sq

        @pl.loop(1, ROOTS)
        def _(d):
            q = lax.rem(here + d, ROOTS)
            to_other(q, q).wait_recv()

        sumsq = jnp.sum(jnp.sum(xbuf[...], axis=0), keepdims=True)
        limit = TARGET_RMS * width * math.sqrt(ROOTS)
        clip = limit / jnp.sqrt(sumsq)
        kappa = (limit * limit / width) * (fb / sumsq)
        c2 = kappa * kappa * norm2 + (2.0 * RIDGE) * kappa * trace + RIDGE * RIDGE * width
        c = jnp.sqrt(c2)
        start = lax.rsqrt(jnp.sqrt(c))
        coefs = [v * start for v in shifted(kappa / c, RIDGE / c)]

        def finish(n, q, k):
            high = (coefs[4] * n + coefs[5] * q + coefs[6] * k).astype(BF16)
            low = coefs[1] * n + coefs[2] * q + coefs[3] * k + jnp.where(eye, coefs[0], 0.0)
            return (low + dot(k.astype(BF16), high, NN)).astype(BF16)

        left_root = finish(left, left2, left3)
        hidden = (clip * dot(left_root, grad, NN)).astype(BF16)
        right_root = finish(right, right2, right3)
        upd[...] = dot(hidden, right_root, NN).reshape(PER_BLOCK, 16, width)

        @pl.loop(1, PER_BLOCK)
        def _(d):
            from_root(lax.rem(mine + d, PER_BLOCK)).start()

        out_ref[...] = upd[mine]

        @pl.loop(1, PER_BLOCK)
        def _(d):
            from_root(lax.rem(mine + d, PER_BLOCK)).wait_send()

        @pl.loop(1, ROOTS)
        def _(d):
            to_other(lax.rem(here + d, ROOTS), here).wait_send()

    @pl.when(jnp.logical_not(is_root))
    def _():
        for copy in to_root(mine):
            copy.wait_send()

    for copy in started:
        copy.wait_send()
    for j in range(PARTS):
        for a in range(3):
            to, copy = across(j, a)

            @pl.when(z != to)
            def _():
                copy.wait_send()

    @pl.when(jnp.logical_not(is_root))
    def _():
        from_root(mine).wait_recv()
        out_ref[...] = land[...]


def body(grad_partials):
    width = grad_partials.shape[-1]
    g = grad_partials.reshape(NY, 3, PARTS, 16, width)
    dma = pltpu.SemaphoreType.DMA
    out = pl.pallas_call(
        kernel,
        out_shape=jax.ShapeDtypeStruct((16, width), F32),
        in_specs=[pl.BlockSpec(memory_space=pl.ANY)],
        out_specs=pl.BlockSpec(memory_space=pltpu.VMEM),
        scratch_shapes=[
            pltpu.VMEM((NY, 3, PARTS, 16, width), BF16),
            pltpu.VMEM((PARTS, 4, 3, 16, width), BF16),
            pltpu.VMEM((PARTS, 4, 3, 16, width), BF16),
            pltpu.VMEM((PARTS, 3, 3, 16, width), BF16),
            pltpu.VMEM((PARTS, 3, 3, 16, width), BF16),
            pltpu.VMEM((PARTS, 3, 16, width), BF16),
            pltpu.VMEM((16, width), F32),
            pltpu.VMEM((NZ, 16, width), BF16),
            pltpu.VMEM((16, width), BF16),
            pltpu.VMEM((8, 128), F32),
            pltpu.VMEM((PER_BLOCK, 16, width), BF16),
            pltpu.VMEM((PER_BLOCK, 8, 128), F32),
            pltpu.VMEM((8, 128), F32),
            pltpu.VMEM((ROOTS, 8, 128), F32),
            pltpu.VMEM((PER_BLOCK, 16, width), F32),
            pltpu.VMEM((16, width), F32),
            dma,
            dma((PARTS, 4)), dma((PARTS, 4)), dma((PARTS, 4)), dma((PARTS, 4)),
            dma((NZ,)), dma((NZ,)),
            dma, dma((PER_BLOCK,)), dma, dma((PER_BLOCK,)),
            dma((ROOTS,)), dma((ROOTS,)), dma((PER_BLOCK,)), dma,
        ],
        compiler_params=pltpu.CompilerParams(
            collective_id=0, has_side_effects=True, vmem_limit_bytes=48 * 2**20
        ),
    )(g)
    return out[None]


def solution(mesh):
    placed = (P("dp", "shard", None, None),)
    return jax.shard_map(
        body, mesh=mesh, in_specs=placed, out_specs=P("shard", "dp", None), check_vma=False
    )
```

time: 1200 us -> 72.7 us (0.06)
  the two profiles are of different devices: /device:TPU:4 before, /device:TPU:73 now
where the time goes in v1:
time: 72.7 us; the launch traced here: 72.6 us
  Pallas kernels  70.5 us (97%)
  local copies, waits for them, and re-layouts  2.02 us (3%)
    pallas_call x1, Pallas kernels, body(): pl.pallas_call(kernel, out_shape=jax.ShapeDtypeStruct((16, width), F32),...  70.5 us
    unnamed x3, local copies, waits for them, and re-layouts  2.02 us

profile of v1, /device:TPU:73, one launch (start us, length us, event | category | flops | bytes accessed | tf_op | source)
XLA Modules:
  0.0 72.6 jit_solution(7823491057433952150)
XLA Ops:
  0.0 0.0 copy-start
  0.0 1.4 %copy-done = bf16[1,1,1536,512]{3,2,1,0:T(8,128)(2,1)S(1)} copy-done((bf16[1,1,1536,512]{3,2,1,0:T(8,128)(2,1)S(1)}, bf16[1,1,1536,512]{3,2,1,0:T(8,128)(2,1)}, u32[]{:S(2)}) %copy-start) | copy-done | bytes 1572888
  1.4 70.5 %shard_map.17 = f32[16,512]{1,0:T(8,128)S(1)} custom-call(bf16[8,3,4,16,512]{4,3,2,1,0:T(8,128)(2,1)S(1)} %bitcast.2), custom_call_target="tpu_custom_call" | custom-call | tf_op jit(solution)/shard_map/pallas_call | solution.py:304
  72.0 0.6 copy.3
Async XLA Ops:
  0.0 1.4 %copy-start = (bf16[1,1,1536,512]{3,2,1,0:T(8,128)(2,1)S(1)}, bf16[1,1,1536,512]{3,2,1,0:T(8,128)(2,1)}, u32[]{:S(2)}) copy-start(bf16[1,1,1536,512]{3,2,1,0:T(8,128)(2,1)} %param.1) | copy-start | bytes 4718596

commit v2 on v1

--- a/solution.py
+++ b/solution.py
@@ -41,7 +41,7 @@
 
 def root_of(block, shard):
     row = 1 + 2 * block + block // 2
-    return row * NZ + lax.rem(shard, 2)
+    return row * NZ + NZ - 1 - 8 * lax.rem(shard, 2)
 
 
 def dot(a, b, dims):
@@ -55,9 +55,9 @@
 
 def kernel(
     g_ref, out_ref,
-    loc, rbuf, lbuf, rsend, lsend, zsend, own, zbuf, piece, sq, gath, gsq, tot, xbuf, upd, land,
-    loc_sem, rs_sem, rr_sem, ls_sem, lr_sem, zs_sem, zr_sem, gs_sem, gr_sem, qs_sem, qr_sem,
-    xs_sem, xr_sem, us_sem, ur_sem,
+    loc, rbuf, lbuf, rsend, lsend, zsend, own, zbuf, piece, sq, gath, peers, line, lines, upd, land,
+    loc_sem, rs_sem, rr_sem, ls_sem, lr_sem, zs_sem, zr_sem, gs_sem, gr_sem, ps_sem, pr_sem,
+    ts_sem, tr_sem, us_sem, ur_sem, known,
 ):
     i = lax.axis_index("dp")
     s = lax.axis_index("shard")
@@ -65,7 +65,6 @@
     block, mine = i // PER_BLOCK, lax.rem(i, PER_BLOCK)
     root = root_of(block, s)
     is_root = i == root
-    here = block * NS + s
 
     def yy(d):
         return lax.rem(y + d + NY, NY)
@@ -90,26 +89,22 @@
     up, down = yy(1) * NZ + z, yy(-1) * NZ + z
     greet(up, s)
     greet(down, s)
-    for d in range(1, NZ):
-        greet(y * NZ + zz(d), s)
-
-    @pl.when(is_root)
-    def _():
-        @pl.loop(1, PER_BLOCK)
-        def _(d):
-            greet(block * PER_BLOCK + lax.rem(mine + d, PER_BLOCK), s)
-
-        @pl.loop(1, ROOTS)
-        def _(d):
-            q = lax.rem(here + d, ROOTS)
-            greet(root_of(q // NS, lax.rem(q, NS)), lax.rem(q, NS))
-
-        pl.semaphore_wait(barrier, 2 + NZ - 1 + PER_BLOCK - 1 + ROOTS - 1)
-
-    @pl.when(jnp.logical_not(is_root))
-    def _():
-        greet(root, s)
-        pl.semaphore_wait(barrier, 2 + NZ - 1 + 1)
+    greet(y * NZ + zz(1), s)
+    greet(y * NZ + zz(-1), s)
+    for d in range(1, NS):
+        greet(i, lax.rem(s + d, NS))
+    pl.semaphore_wait(barrier, 4 + NS - 1)
+
+    def tell(stage):
+        for side, sign in ((0, 1), (1, -1)):
+            pl.semaphore_signal(
+                known.at[stage, side], inc=1,
+                device_id=(y * NZ + zz(sign * 2**stage), s), device_id_type=MESH,
+            )
+
+    def hear(stage):
+        pl.semaphore_wait(known.at[stage, 0], 1)
+        pl.semaphore_wait(known.at[stage, 1], 1)
 
     def count(way, j):
         return 4 if (j < PARTS // 2) == (way > 0) else 3
@@ -123,6 +118,10 @@
         return remote(src, buf.at[j, t], ssem.at[j, t], rsem.at[j, t], (up if way > 0 else down, s))
 
     for t in range(4):
+        if t > 1:
+            hear(t - 2)
+        if t > 0:
+            tell(t - 1)
         for j in range(PARTS):
             for way in (1, -1):
                 if t >= count(way, j):
@@ -147,6 +146,7 @@
             zr_sem.at[lax.rem(to - z + NZ, NZ)], (y * NZ + to, s),
         )
 
+    hear(2)
     for j in range(PARTS):
         ring(1, j, count(1, j) - 1).wait_recv()
         ring(-1, j, count(-1, j) - 1).wait_recv()
@@ -177,15 +177,33 @@
     folded = squares[0:8] + squares[8:16]
     sq[...] = folded[:, 0:128] + folded[:, 128:256] + folded[:, 256:384] + folded[:, 384:512]
 
+    def to_peer(d):
+        return remote(sq, peers.at[d], ps_sem.at[d], pr_sem.at[d], (i, lax.rem(s + d, NS)))
+
+    for d in range(1, NS):
+        to_peer(d).start()
+
     def to_root(slot):
-        return (
-            remote(piece, gath.at[slot], gs_sem, gr_sem.at[slot], (root, s)),
-            remote(sq, gsq.at[slot], qs_sem, qr_sem.at[slot], (root, s)),
-        )
+        return remote(piece, gath.at[slot], gs_sem, gr_sem, (root, s))
 
     @pl.when(jnp.logical_not(is_root))
     def _():
-        for copy in to_root(mine):
+        to_root(mine).start()
+
+    row_sq = sq[...]
+    for d in range(1, NS):
+        to_peer(d).wait_recv()
+        row_sq = row_sq + peers[d]
+    line[...] = row_sq
+
+    def to_column(b, slot):
+        return remote(line, lines.at[slot], ts_sem.at[b], tr_sem, (root_of(b, s), s))
+
+    for b in range(BLOCKS):
+        copy = to_column(b, i)
+
+        @pl.when(i != root_of(b, s))
+        def _():
             copy.start()
 
     def from_root(m):
@@ -196,36 +214,22 @@
     @pl.when(is_root)
     def _():
         gath[mine] = piece[...]
-        gsq[mine] = sq[...]
-
-        @pl.loop(1, PER_BLOCK)
-        def _(d):
-            for copy in to_root(lax.rem(mine + d, PER_BLOCK)):
-                copy.wait_recv()
-
-        block_sq = jnp.sum(gsq[...], axis=0)
-        tot[...] = block_sq
-
-        def to_other(q, slot):
-            return remote(
-                tot, xbuf.at[slot], xs_sem.at[q], xr_sem.at[slot],
-                (root_of(q // NS, lax.rem(q, NS)), lax.rem(q, NS)),
-            )
-
-        @pl.loop(1, ROOTS)
-        def _(d):
-            to_other(lax.rem(here + d, ROOTS), here).start()
+        lines[i] = row_sq
+        remote(
+            gath.at[pl.ds(0, PER_BLOCK - 1)], gath.at[pl.ds(0, PER_BLOCK - 1)], gs_sem, gr_sem, (up, s)
+        ).wait_recv()
 
         width = 16 * PER_BLOCK
         grad = gath[...].reshape(width, width)
-        fb = jnp.sum(block_sq, keepdims=True)
+        wide = grad.astype(F32)
+        fb = jnp.sum(wide * wide, keepdims=True)
         inverse = jnp.where(fb > 0.0, 1.0 / fb, 0.0)
         left = dot(grad, grad, NT) * inverse
         right = dot(grad, grad, TN) * inverse
         eye = lax.broadcasted_iota(jnp.int32, (width, width), 0) == lax.broadcasted_iota(
             jnp.int32, (width, width), 1
         )
-        trace = jnp.sum(jnp.where(eye, left, 0.0), keepdims=True)
+        trace = jnp.where(fb > 0.0, 1.0, 0.0)
         norm2 = jnp.sum(left * left, keepdims=True)
 
         def powers(n):
@@ -236,14 +240,12 @@
         left2, left3 = powers(left)
         right2, right3 = powers(right)
 
-        xbuf[here] = block_sq
-
-        @pl.loop(1, ROOTS)
-        def _(d):
-            q = lax.rem(here + d, ROOTS)
-            to_other(q, q).wait_recv()
-
-        sumsq = jnp.sum(jnp.sum(xbuf[...], axis=0), keepdims=True)
+        others = NY * NZ - 1
+        remote(
+            lines.at[pl.ds(0, others)], lines.at[pl.ds(0, others)], gs_sem, tr_sem, (up, s)
+        ).wait_recv()
+
+        sumsq = jnp.sum(jnp.sum(lines[...], axis=0), keepdims=True)
         limit = TARGET_RMS * width * math.sqrt(ROOTS)
         clip = limit / jnp.sqrt(sumsq)
         kappa = (limit * limit / width) * (fb / sumsq)
@@ -262,9 +264,15 @@
         right_root = finish(right, right2, right3)
         upd[...] = dot(hidden, right_root, NN).reshape(PER_BLOCK, 16, width)
 
-        @pl.loop(1, PER_BLOCK)
-        def _(d):
-            from_root(lax.rem(mine + d, PER_BLOCK)).start()
+        first = 5 * block // 2
+
+        @pl.loop(0, 4 * NZ)
+        def _(k):
+            m = (first + lax.rem(k, 4)) * NZ + k // 4 - block * PER_BLOCK
+
+            @pl.when(jnp.logical_and(jnp.logical_and(m >= 0, m < PER_BLOCK), m != mine))
+            def _():
+                from_root(m).start()
 
         out_ref[...] = upd[mine]
 
@@ -272,13 +280,17 @@
         def _(d):
             from_root(lax.rem(mine + d, PER_BLOCK)).wait_send()
 
-        @pl.loop(1, ROOTS)
-        def _(d):
-            to_other(lax.rem(here + d, ROOTS), here).wait_send()
-
     @pl.when(jnp.logical_not(is_root))
     def _():
-        for copy in to_root(mine):
+        to_root(mine).wait_send()
+
+    for d in range(1, NS):
+        to_peer(d).wait_send()
+    for b in range(BLOCKS):
+        copy = to_column(b, i)
+
+        @pl.when(i != root_of(b, s))
+        def _():
             copy.wait_send()
 
     for copy in started:
@@ -318,16 +330,17 @@
             pltpu.VMEM((16, width), BF16),
             pltpu.VMEM((8, 128), F32),
             pltpu.VMEM((PER_BLOCK, 16, width), BF16),
-            pltpu.VMEM((PER_BLOCK, 8, 128), F32),
+            pltpu.VMEM((NS, 8, 128), F32),
             pltpu.VMEM((8, 128), F32),
-            pltpu.VMEM((ROOTS, 8, 128), F32),
+            pltpu.VMEM((NY * NZ, 8, 128), F32),
             pltpu.VMEM((PER_BLOCK, 16, width), F32),
             pltpu.VMEM((16, width), F32),
             dma,
             dma((PARTS, 4)), dma((PARTS, 4)), dma((PARTS, 4)), dma((PARTS, 4)),
             dma((NZ,)), dma((NZ,)),
-            dma, dma((PER_BLOCK,)), dma, dma((PER_BLOCK,)),
-            dma((ROOTS,)), dma((ROOTS,)), dma((PER_BLOCK,)), dma,
+            dma, dma, dma((NS,)), dma((NS,)),
+            dma((BLOCKS,)), dma, dma((PER_BLOCK,)), dma,
+            pltpu.SemaphoreType.REGULAR((3, 2)),
         ],
         compiler_params=pltpu.CompilerParams(
             collective_id=0, has_side_effects=True, vmem_limit_bytes=48 * 2**20

time: 72.7 us -> 63.8 us (0.88)
  the two profiles are of different devices: /device:TPU:73 before, /device:TPU:256 now
where the time goes in v2:
time: 63.8 us; the launch traced here: 63.6 us
  Pallas kernels  61.6 us (97%)
  local copies, waits for them, and re-layouts  2.02 us (3%)
    pallas_call x1, Pallas kernels, body(): pl.pallas_call(kernel, out_shape=jax.ShapeDtypeStruct((16, width), F32),...  61.6 us
    unnamed x3, local copies, waits for them, and re-layouts  2.02 us

profile of v2, /device:TPU:256, one launch (start us, length us, event | category | flops | bytes accessed | tf_op | source)
XLA Modules:
  0.0 63.6 jit_solution(13769655390079213188)
XLA Ops:
  0.0 0.0 copy-start
  0.0 1.4 %copy-done = bf16[1,1,1536,512]{3,2,1,0:T(8,128)(2,1)S(1)} copy-done((bf16[1,1,1536,512]{3,2,1,0:T(8,128)(2,1)S(1)}, bf16[1,1,1536,512]{3,2,1,0:T(8,128)(2,1)}, u32[]{:S(2)}) %copy-start) | copy-done | bytes 1572888
  1.4 61.6 %shard_map.17 = f32[16,512]{1,0:T(8,128)S(1)} custom-call(bf16[8,3,4,16,512]{4,3,2,1,0:T(8,128)(2,1)S(1)} %bitcast.2), custom_call_target="tpu_custom_call" | custom-call | tf_op jit(solution)/shard_map/pallas_call | solution.py:316
  63.0 0.6 copy.3
Async XLA Ops:
  0.0 1.4 %copy-start = (bf16[1,1,1536,512]{3,2,1,0:T(8,128)(2,1)S(1)}, bf16[1,1,1536,512]{3,2,1,0:T(8,128)(2,1)}, u32[]{:S(2)}) copy-start(bf16[1,1,1536,512]{3,2,1,0:T(8,128)(2,1)} %param.1) | copy-start | bytes 4718596

commit v3 on v2

v3 whole, which is shorter than its diff:
```python
import functools
import math

import jax
import jax.numpy as jnp
from jax import lax
from jax.experimental import pallas as pl
from jax.experimental.pallas import tpu as pltpu
from jax.sharding import PartitionSpec as P

MESH = pl.DeviceIdType.MESH
NY, NZ, NS = 8, 12, 8
PARTS = 4
NARROW = 128
PER_BLOCK = 32
BLOCKS = 3
SPANS = 3
RIDGE = 0.1
TARGET_RMS = 0.5
F32, BF16 = jnp.float32, jnp.bfloat16


def series():
    coefs = [25.0 / 16.0, -5.0 / 16.0, 0.0, 0.0, 0.0, 0.0, 0.0]
    for power in range(6):
        coefs[power + 1] -= math.comb(5, power) * 5.0 ** (5 - power) * (-1.0) ** power / 4096.0
    return coefs


def shifted(beta, gamma):
    coefs = series()
    out = []
    scale = jnp.ones_like(beta)
    for j in range(7):
        total = jnp.zeros_like(beta)
        for i in range(6, j - 1, -1):
            total = total * gamma + coefs[i] * math.comb(i, j)
        out.append(total * scale)
        scale = scale * beta
    return out


def root_of(block, shard, k):
    row = 1 + 2 * block + block // 2
    return row * NZ + lax.rem(NZ - 1 + 2 * lax.rem(shard, 2) + 4 * k, NZ)


def dot(a, b, dims):
    return lax.dot_general(a, b, (dims, ((), ())), preferred_element_type=F32)


NN = ((1,), (0,))
TN = ((0,), (0,))


def kernel(
    g_ref, out_ref,
    loc, pick, rbuf, lbuf, rsend, lsend, zsend, own, zbuf, araw, asum, afin, asend, abuf, piece, sq, gath, peers, line, lines, upd, land,
    loc_sem, rs_sem, rr_sem, ls_sem, lr_sem, zs_sem, zr_sem, gs_sem, gr_sem, ps_sem, pr_sem,
    ts_sem, tr_sem, us_sem, ur_sem, known, along,
    as_sem, ar_sem, bs_sem, br_sem, cs_sem, cr_sem,
):
    i = lax.axis_index("dp")
    s = lax.axis_index("shard")
    y, z = i // NZ, lax.rem(i, NZ)
    block, mine = i // PER_BLOCK, lax.rem(i, PER_BLOCK)
    ahead = lax.rem(z + NZ + 2 - 2 * lax.rem(s, 2), NZ)
    span = ahead // 4
    is_root = functools.reduce(jnp.logical_or, [i == root_of(block, s, k) for k in range(SPANS)])

    def yy(d):
        return lax.rem(y + d + NY, NY)

    def zz(d):
        return lax.rem(z + d + NZ, NZ)

    def remote(src, dst, ssem, rsem, dev):
        return pltpu.make_async_remote_copy(
            src_ref=src, dst_ref=dst, send_sem=ssem, recv_sem=rsem,
            device_id=dev, device_id_type=MESH,
        )

    local = pltpu.make_async_copy(g_ref, loc, loc_sem)
    local.start()

    barrier = pltpu.get_barrier_semaphore()

    def greet(dp, shard):
        pl.semaphore_signal(barrier, inc=1, device_id=(dp, shard), device_id_type=MESH)

    up, down = yy(1) * NZ + z, yy(-1) * NZ + z
    for d in (1, -1, 2, -2):
        greet(yy(d) * NZ + z, s)
        greet(y * NZ + zz(d), s)
    for d in range(1, NS):
        greet(i, lax.rem(s + d, NS))
    pl.semaphore_wait(barrier, 8 + NS - 1)

    def tell(stage):
        for side, step in ((0, 2 << stage), (1, -(2 << stage))):
            pl.semaphore_signal(
                known.at[stage, side], inc=1, device_id=(y * NZ + zz(step), s), device_id_type=MESH
            )
            if stage == 0:
                pl.semaphore_signal(
                    along.at[side], inc=1, device_id=(yy(step) * NZ + z, s), device_id_type=MESH
                )

    def hear(stage):
        for side in range(2):
            pl.semaphore_wait(known.at[stage, side], 1)
            if stage == 0:
                pl.semaphore_wait(along.at[side], 1)

    wide = pl.ds(NARROW, g_ref.shape[-1] - NARROW)

    def stretch(j):
        return lax.rem(z // 3 + (2, 1, 3, 0)[j], PARTS)

    def count(way, j):
        return 4 if (j < PARTS // 2) == (way > 0) else 3

    tables = {1: (rbuf, rsend, rs_sem, rr_sem), -1: (lbuf, lsend, ls_sem, lr_sem)}
    started = []

    def begin(copy):
        copy.start()
        started.append(copy)

    def ring(way, j, t):
        buf, sends, ssem, rsem = tables[way]
        src = g_ref.at[yy(way * count(way, j)), stretch(j), :, :, wide] if t == 0 else sends.at[j, t - 1]
        return remote(src, buf.at[j, t], ssem.at[j, t], rsem.at[j, t], (up if way > 0 else down, s))

    def ring_step(t):
        for j in range(PARTS):
            for way in (1, -1):
                if t >= count(way, j):
                    continue
                if t > 0:
                    buf, sends, _, _ = tables[way]
                    ring(way, j, t - 1).wait_recv()
                    chunk = yy(way * (count(way, j) - t))
                    sends[j, t - 1] = (
                        loc[chunk, stretch(j), :, :, wide].astype(F32) + buf[j, t - 1].astype(F32)
                    ).astype(BF16)
                begin(ring(way, j, t))

    narrow = pl.ds(0, NARROW)
    raw_far, sum_far = ((6, 4, 2), (5, 3)), ((5, 3, 1), (4, 2))

    def sign(h, side):
        return 1 if h == side else -1

    def part(ref, h, chunk):
        return ref.at[pl.ds(4 * h, 4), chunk // 3, lax.rem(chunk, 3), :, narrow]

    def raw(h, side, n):
        to = zz(sign(h, side))
        return remote(
            part(g_ref, h, zz(sign(h, side) * raw_far[side][n])), araw.at[h, side, n],
            as_sem.at[h, side, n], ar_sem.at[h, side, n], (y * NZ + to, s),
        )

    def paired(h, side, n):
        if n == 2 and side == 1:
            to = zz(sign(h, side))
            src = part(g_ref, h, to)
        else:
            to = zz(sign(h, side) * sum_far[side][n])
            src = asum.at[h, side, n]
        return remote(
            src, afin.at[h, side, n], bs_sem.at[h, side, n], br_sem.at[h, side, n], (y * NZ + to, s)
        )

    def pair_step(h, side, n):
        raw(h, side, n).wait_recv()
        to = zz(sign(h, side) * sum_far[side][n])
        asum[h, side, n] = (
            part(loc, h, to)[...].astype(F32) + araw[h, side, n].astype(F32)
        ).astype(BF16)
        begin(paired(h, side, n))

    tell(0)
    ring_step(0)
    for n in range(3):
        for h in range(2):
            for side in range(2):
                if n < len(raw_far[side]):
                    begin(raw(h, side, n))
    for h in range(2):
        begin(paired(h, 1, 2))
    local.wait()
    ring_step(1)
    hear(0)
    tell(1)
    for side, n in ((1, 0), (0, 1), (1, 1), (0, 2)):
        for h in range(2):
            pair_step(h, side, n)
    ring_step(2)
    hear(1)
    for h in range(2):
        pair_step(h, 0, 0)
    ring_step(3)

    def to_row(d):
        to = yy(d)
        return remote(asend.at[to], abuf.at[d], cs_sem.at[d], cr_sem.at[d], (to * NZ + z, s))

    for h in range(2):
        narrow_sum = part(loc, h, z)[...].astype(F32)
        for n in range(3):
            for side in range(2):
                paired(h, side, n).wait_recv()
                narrow_sum = narrow_sum + afin[h, side, n].astype(F32)
        asend[pl.ds(4 * h, 4)] = narrow_sum
    for d in range(1, NY):
        begin(to_row(d))

    def across(j, a):
        to = 3 * stretch(j) + a
        slot = lax.rem(to - z + NZ, NZ)
        return to, remote(
            zsend.at[j, a], zbuf.at[slot], zs_sem.at[j, a], zr_sem.at[slot], (y * NZ + to, s)
        )

    for j in range(PARTS):
        ring(1, j, count(1, j) - 1).wait_recv()
        ring(-1, j, count(-1, j) - 1).wait_recv()
        total = (
            loc[y, stretch(j), :, :, wide].astype(F32)
            + rbuf[j, count(1, j) - 1].astype(F32)
            + lbuf[j, count(-1, j) - 1].astype(F32)
        )
        zsend[j] = total.astype(BF16)
        for a in range(3):
            to, copy = across(j, a)

            @pl.when(z != to)
            def _():
                copy.start()

            @pl.when(z == to)
            def _():
                own[...] = total[a]

    left_rows = asend[y]
    for d in range(1, NY):
        to_row(d).wait_recv()
        left_rows = left_rows + abuf[d]
    right_rows = own[...]
    for d in range(1, NZ):
        remote(zsend.at[0, 0], zbuf.at[d], zs_sem.at[0, 0], zr_sem.at[d], (up, s)).wait_recv()
        right_rows = right_rows + zbuf[d].astype(F32)

    piece[:, 0:NARROW] = left_rows.astype(BF16)
    piece[:, NARROW:] = right_rows.astype(BF16)
    folded = jnp.zeros((16, 128), F32)
    for side_rows in (left_rows, right_rows):
        for k in range(side_rows.shape[1] // 128):
            square = side_rows[:, k * 128 : (k + 1) * 128]
            folded = folded + square * square
    sq[...] = jnp.sum(folded, axis=0, keepdims=True)

    def to_peer(d):
        return remote(sq, peers.at[d], ps_sem.at[d], pr_sem.at[d], (i, lax.rem(s + d, NS)))

    for d in range(1, NS):
        to_peer(d).start()

    def to_root(k, slot):
        return remote(piece, gath.at[slot], gs_sem.at[k], gr_sem, (root_of(block, s, k), s))

    for k in range(SPANS):
        copy = to_root(k, mine)

        @pl.when(i != root_of(block, s, k))
        def _():
            copy.start()

    row_sq = sq[...]
    for d in range(1, NS):
        to_peer(d).wait_recv()
        row_sq = row_sq + peers[d]
    line[...] = row_sq

    def to_column(b, k, slot):
        return remote(
            line, lines.at[slot], ts_sem.at[b, k], tr_sem, (root_of(b, s, k), s)
        )

    for b in range(BLOCKS):
        for k in range(SPANS):
            copy = to_column(b, k, i)

            @pl.when(i != root_of(b, s, k))
            def _():
                copy.start()

    @pl.when(is_root)
    def _():
        gath[mine] = piece[...]
        lines[i] = row_sq
        remote(
            gath.at[pl.ds(0, PER_BLOCK - 1)], gath.at[pl.ds(0, PER_BLOCK - 1)], us_sem.at[0], gr_sem, (up, s)
        ).wait_recv()

        width = 16 * PER_BLOCK
        grad = gath[...].reshape(width, width)
        exact = grad.astype(F32)
        fb = jnp.sum(exact * exact, keepdims=True)
        inverse = jnp.where(fb > 0.0, 1.0 / fb, 0.0)
        n1 = dot(grad, grad, TN) * inverse
        eye = lax.broadcasted_iota(jnp.int32, (width, width), 0) == lax.broadcasted_iota(
            jnp.int32, (width, width), 1
        )
        trace = jnp.where(fb > 0.0, 1.0, 0.0)
        norm2 = jnp.sum(n1 * n1, keepdims=True)
        nb = n1.astype(BF16)
        n2 = dot(nb, nb, NN)
        n3 = dot(nb, n2.astype(BF16), NN)

        first = 5 * block // 2

        def served(k):
            at = lax.rem(NZ - 2 + 2 * lax.rem(s, 2) + 4 * span + lax.rem(k // 4 + 2, 4), NZ)
            m = (first + lax.rem(k, 4)) * NZ + at - block * PER_BLOCK
            return m, jnp.logical_and(jnp.logical_and(m >= 0, m < PER_BLOCK), m != mine)

        for k in range(16):
            pick[k] = gath[lax.rem(served(k)[0] + PER_BLOCK, PER_BLOCK)]

        others = NY * NZ - 1
        remote(
            lines.at[pl.ds(0, others)], lines.at[pl.ds(0, others)], us_sem.at[0], tr_sem, (up, s)
        ).wait_recv()

        sumsq = jnp.sum(jnp.sum(lines[...], axis=0), keepdims=True)
        limit = TARGET_RMS * width * math.sqrt(BLOCKS * NS)
        clip = limit / jnp.sqrt(sumsq)
        kappa = (limit * limit / width) * (fb / sumsq)
        c2 = kappa * kappa * norm2 + (2.0 * RIDGE) * kappa * trace + RIDGE * RIDGE * width
        c = jnp.sqrt(c2)
        start = lax.rsqrt(jnp.sqrt(c))
        coefs = [v * start for v in shifted(kappa / c, RIDGE / c)]

        high = (coefs[4] * n1 + coefs[5] * n2 + coefs[6] * n3).astype(BF16)
        low = coefs[1] * n1 + coefs[2] * n2 + coefs[3] * n3 + jnp.where(eye, coefs[0], 0.0)
        root = (low + dot(n3.astype(BF16), high, NN)).astype(BF16)
        rows = pick[...].reshape(16 * 16, width)
        hidden = (clip * dot(rows, root, NN)).astype(BF16)
        upd[...] = dot(hidden, root, NN).reshape(16, 16, width)

        def from_root(k, m):
            return remote(upd.at[k], land, us_sem.at[k], ur_sem, (block * PER_BLOCK + m, s))

        @pl.loop(0, 16)
        def _(k):
            m, other = served(k)

            @pl.when(other)
            def _():
                from_root(k, m).start()

        out_ref[...] = upd[4 * lax.rem(lax.rem(ahead, 4) + 2, 4) + y - first]

        @pl.loop(0, 16)
        def _(k):
            m, other = served(k)

            @pl.when(other)
            def _():
                from_root(k, m).wait_send()

    for k in range(SPANS):
        copy = to_root(k, mine)

        @pl.when(i != root_of(block, s, k))
        def _():
            copy.wait_send()

    for d in range(1, NS):
        to_peer(d).wait_send()
    for b in range(BLOCKS):
        for k in range(SPANS):
            copy = to_column(b, k, i)

            @pl.when(i != root_of(b, s, k))
            def _():
                copy.wait_send()

    for copy in started:
        copy.wait_send()
    for j in range(PARTS):
        for a in range(3):
            to, copy = across(j, a)

            @pl.when(z != to)
            def _():
                copy.wait_send()

    @pl.when(jnp.logical_not(is_root))
    def _():
        remote(upd.at[0], land, us_sem.at[0], ur_sem, (up, s)).wait_recv()
        out_ref[...] = land[...]


def body(grad_partials):
    width = grad_partials.shape[-1]
    g = grad_partials.reshape(NY, PARTS, 3, 16, width)
    dma = pltpu.SemaphoreType.DMA
    rest = width - NARROW
    out = pl.pallas_call(
        kernel,
        out_shape=jax.ShapeDtypeStruct((16, width), F32),
        in_specs=[pl.BlockSpec(memory_space=pltpu.HBM)],
        out_specs=pl.BlockSpec(memory_space=pltpu.VMEM),
        scratch_shapes=[
            pltpu.VMEM((NY, PARTS, 3, 16, width), BF16),
            pltpu.VMEM((16, 16, width), BF16),
            pltpu.VMEM((PARTS, 4, 3, 16, rest), BF16),
            pltpu.VMEM((PARTS, 4, 3, 16, rest), BF16),
            pltpu.VMEM((PARTS, 3, 3, 16, rest), BF16),
            pltpu.VMEM((PARTS, 3, 3, 16, rest), BF16),
            pltpu.VMEM((PARTS, 3, 16, rest), BF16),
            pltpu.VMEM((16, rest), F32),
            pltpu.VMEM((NZ, 16, rest), BF16),
            pltpu.VMEM((2, 2, 3, 4, 16, NARROW), BF16),
            pltpu.VMEM((2, 2, 3, 4, 16, NARROW), BF16),
            pltpu.VMEM((2, 2, 3, 4, 16, NARROW), BF16),
            pltpu.VMEM((NY, 16, NARROW), F32),
            pltpu.VMEM((NY, 16, NARROW), F32),
            pltpu.VMEM((16, width), BF16),
            pltpu.VMEM((1, 128), F32),
            pltpu.VMEM((PER_BLOCK, 16, width), BF16),
            pltpu.VMEM((NS, 1, 128), F32),
            pltpu.VMEM((1, 128), F32),
            pltpu.VMEM((NY * NZ, 1, 128), F32),
            pltpu.VMEM((16, 16, width), F32),
            pltpu.VMEM((16, width), F32),
            dma,
            dma((PARTS, 4)), dma((PARTS, 4)), dma((PARTS, 4)), dma((PARTS, 4)),
            dma((PARTS, 3)), dma((NZ,)),
            dma((SPANS,)), dma, dma((NS,)), dma((NS,)),
            dma((BLOCKS, SPANS)), dma, dma((16,)), dma,
            pltpu.SemaphoreType.REGULAR((2, 2)),
            pltpu.SemaphoreType.REGULAR((2,)),
            dma((2, 2, 3)), dma((2, 2, 3)), dma((2, 2, 3)), dma((2, 2, 3)), dma((NY,)), dma((NY,)),
        ],
        compiler_params=pltpu.CompilerParams(
            collective_id=0, has_side_effects=True, vmem_limit_bytes=48 * 2**20
        ),
    )(g)
    return out[None]


def solution(mesh):
    placed = (P("dp", "shard", None, None),)
    return jax.shard_map(
        body, mesh=mesh, in_specs=placed, out_specs=P("shard", "dp", None), check_vma=False
    )
```

time: 63.8 us -> 60.3 us (0.945)
  the two profiles are of different devices: /device:TPU:256 before, /device:TPU:64 now
where the time goes in v3:
time: 60.3 us; the launch traced here: 60.2 us
  Pallas kernels  58.1 us (96%)
  local copies, waits for them, and re-layouts  2.02 us (3%)
    pallas_call x1, Pallas kernels, body(): pl.pallas_call(kernel, out_shape=jax.ShapeDtypeStruct((16, width), F32),...  58.1 us
    unnamed x3, local copies, waits for them, and re-layouts  2.02 us

profile of v3, /device:TPU:64, one launch (start us, length us, event | category | flops | bytes accessed | tf_op | source)
XLA Modules:
  0.0 60.2 jit_solution(16390463862640011502)
XLA Ops:
  0.0 0.0 copy-start
  0.0 1.4 %copy-done = bf16[1,1,1536,512]{3,2,1,0:T(8,128)(2,1)S(1)} copy-done((bf16[1,1,1536,512]{3,2,1,0:T(8,128)(2,1)S(1)}, bf16[1,1,1536,512]{3,2,1,0:T(8,128)(2,1)}, u32[]{:S(2)}) %copy-start) | copy-done | bytes 1572888
  1.4 58.1 %shard_map.17 = f32[16,512]{1,0:T(8,128)S(1)} custom-call(bf16[8,4,3,16,512]{4,3,2,1,0:T(8,128)(2,1)S(1)} %bitcast.2), custom_call_target="tpu_custom_call" | custom-call | tf_op jit(solution)/shard_map/pallas_call | solution.py:413
  59.6 0.6 %copy.3 = f32[1,16,512]{2,1,0:T(8,128)} copy(f32[1,16,512]{2,1,0:T(8,128)S(1)} %bitcast.3) | data formatting | bytes 65536
Async XLA Ops:
  0.0 1.4 %copy-start = (bf16[1,1,1536,512]{3,2,1,0:T(8,128)(2,1)S(1)}, bf16[1,1,1536,512]{3,2,1,0:T(8,128)(2,1)}, u32[]{:S(2)}) copy-start(bf16[1,1,1536,512]{3,2,1,0:T(8,128)(2,1)} %param.1) | copy-start | bytes 4718596

commit v4 on v3

--- a/solution.py
+++ b/solution.py
@@ -42,7 +42,7 @@
 
 def root_of(block, shard, k):
     row = 1 + 2 * block + block // 2
-    return row * NZ + lax.rem(NZ - 1 + 2 * lax.rem(shard, 2) + 4 * k, NZ)
+    return row * NZ + lax.rem(shard, 2) + 4 * k
 
 
 def dot(a, b, dims):
@@ -64,7 +64,7 @@
     s = lax.axis_index("shard")
     y, z = i // NZ, lax.rem(i, NZ)
     block, mine = i // PER_BLOCK, lax.rem(i, PER_BLOCK)
-    ahead = lax.rem(z + NZ + 2 - 2 * lax.rem(s, 2), NZ)
+    ahead = lax.rem(z + NZ + 1 - lax.rem(s, 2), NZ)
     span = ahead // 4
     is_root = functools.reduce(jnp.logical_or, [i == root_of(block, s, k) for k in range(SPANS)])
 
@@ -323,7 +323,8 @@
         first = 5 * block // 2
 
         def served(k):
-            at = lax.rem(NZ - 2 + 2 * lax.rem(s, 2) + 4 * span + lax.rem(k // 4 + 2, 4), NZ)
+            turn = lax.rem(k // 4 + 1 - lax.rem(s, 2), 4)
+            at = lax.rem(NZ - 1 + lax.rem(s, 2) + 4 * span + turn, NZ)
             m = (first + lax.rem(k, 4)) * NZ + at - block * PER_BLOCK
             return m, jnp.logical_and(jnp.logical_and(m >= 0, m < PER_BLOCK), m != mine)
 
@@ -362,7 +363,7 @@
             def _():
                 from_root(k, m).start()
 
-        out_ref[...] = upd[4 * lax.rem(lax.rem(ahead, 4) + 2, 4) + y - first]
+        out_ref[...] = upd[4 * lax.rem(lax.rem(ahead, 4) + 3 + lax.rem(s, 2), 4) + y - first]
 
         @pl.loop(0, 16)
         def _(k):

time: 60.3 us -> 59.4 us (0.985)
  the two profiles are of different devices: /device:TPU:64 before, /device:TPU:8 now
where the time goes in v4:
time: 59.4 us; the launch traced here: 59.3 us
  Pallas kernels  57.2 us (96%)
  local copies, waits for them, and re-layouts  2.02 us (3%)
    pallas_call x1, Pallas kernels, body(): pl.pallas_call(kernel, out_shape=jax.ShapeDtypeStruct((16, width), F32),...  57.2 us
    unnamed x3, local copies, waits for them, and re-layouts  2.02 us

profile of v4, /device:TPU:8, one launch (start us, length us, event | category | flops | bytes accessed | tf_op | source)
XLA Modules:
  0.0 59.3 jit_solution(5962287261298223009)
XLA Ops:
  0.0 0.0 copy-start
  0.0 1.4 %copy-done = bf16[1,1,1536,512]{3,2,1,0:T(8,128)(2,1)S(1)} copy-done((bf16[1,1,1536,512]{3,2,1,0:T(8,128)(2,1)S(1)}, bf16[1,1,1536,512]{3,2,1,0:T(8,128)(2,1)}, u32[]{:S(2)}) %copy-start) | copy-done | bytes 1572888
  1.4 57.2 %shard_map.17 = f32[16,512]{1,0:T(8,128)S(1)} custom-call(bf16[8,4,3,16,512]{4,3,2,1,0:T(8,128)(2,1)S(1)} %bitcast.2), custom_call_target="tpu_custom_call" | custom-call | tf_op jit(solution)/shard_map/pallas_call | solution.py:414
  58.6 0.6 %copy.3 = f32[1,16,512]{2,1,0:T(8,128)} copy(f32[1,16,512]{2,1,0:T(8,128)S(1)} %bitcast.3) | data formatting | bytes 65536
Async XLA Ops:
  0.0 1.4 %copy-start = (bf16[1,1,1536,512]{3,2,1,0:T(8,128)(2,1)S(1)}, bf16[1,1,1536,512]{3,2,1,0:T(8,128)(2,1)}, u32[]{:S(2)}) copy-start(bf16[1,1,1536,512]{3,2,1,0:T(8,128)(2,1)} %param.1) | copy-start | bytes 4718596

commit v5 on v4

--- a/solution.py
+++ b/solution.py
@@ -10,7 +10,8 @@
 
 MESH = pl.DeviceIdType.MESH
 NY, NZ, NS = 8, 12, 8
-PARTS = 4
+PARTS = 6
+PER = NZ // PARTS
 NARROW = 128
 PER_BLOCK = 32
 BLOCKS = 3
@@ -115,7 +116,7 @@
     wide = pl.ds(NARROW, g_ref.shape[-1] - NARROW)
 
     def stretch(j):
-        return lax.rem(z // 3 + (2, 1, 3, 0)[j], PARTS)
+        return lax.rem(z // PER + (3, 2, 4, 1, 5, 0)[j], PARTS)
 
     def count(way, j):
         return 4 if (j < PARTS // 2) == (way > 0) else 3
@@ -153,7 +154,7 @@
         return 1 if h == side else -1
 
     def part(ref, h, chunk):
-        return ref.at[pl.ds(4 * h, 4), chunk // 3, lax.rem(chunk, 3), :, narrow]
+        return ref.at[pl.ds(4 * h, 4), chunk // PER, lax.rem(chunk, PER), :, narrow]
 
     def raw(h, side, n):
         to = zz(sign(h, side))
@@ -218,7 +219,7 @@
         begin(to_row(d))
 
     def across(j, a):
-        to = 3 * stretch(j) + a
+        to = PER * stretch(j) + a
         slot = lax.rem(to - z + NZ, NZ)
         return to, remote(
             zsend.at[j, a], zbuf.at[slot], zs_sem.at[j, a], zr_sem.at[slot], (y * NZ + to, s)
@@ -233,7 +234,7 @@
             + lbuf[j, count(-1, j) - 1].astype(F32)
         )
         zsend[j] = total.astype(BF16)
-        for a in range(3):
+        for a in range(PER):
             to, copy = across(j, a)
 
             @pl.when(z != to)
@@ -393,7 +394,7 @@
     for copy in started:
         copy.wait_send()
     for j in range(PARTS):
-        for a in range(3):
+        for a in range(PER):
             to, copy = across(j, a)
 
             @pl.when(z != to)
@@ -408,7 +409,7 @@
 
 def body(grad_partials):
     width = grad_partials.shape[-1]
-    g = grad_partials.reshape(NY, PARTS, 3, 16, width)
+    g = grad_partials.reshape(NY, PARTS, PER, 16, width)
     dma = pltpu.SemaphoreType.DMA
     rest = width - NARROW
     out = pl.pallas_call(
@@ -417,13 +418,13 @@
         in_specs=[pl.BlockSpec(memory_space=pltpu.HBM)],
         out_specs=pl.BlockSpec(memory_space=pltpu.VMEM),
         scratch_shapes=[
-            pltpu.VMEM((NY, PARTS, 3, 16, width), BF16),
+            pltpu.VMEM((NY, PARTS, PER, 16, width), BF16),
             pltpu.VMEM((16, 16, width), BF16),
-            pltpu.VMEM((PARTS, 4, 3, 16, rest), BF16),
-            pltpu.VMEM((PARTS, 4, 3, 16, rest), BF16),
-            pltpu.VMEM((PARTS, 3, 3, 16, rest), BF16),
-            pltpu.VMEM((PARTS, 3, 3, 16, rest), BF16),
-            pltpu.VMEM((PARTS, 3, 16, rest), BF16),
+            pltpu.VMEM((PARTS, 4, PER, 16, rest), BF16),
+            pltpu.VMEM((PARTS, 4, PER, 16, rest), BF16),
+            pltpu.VMEM((PARTS, 3, PER, 16, rest), BF16),
+            pltpu.VMEM((PARTS, 3, PER, 16, rest), BF16),
+            pltpu.VMEM((PARTS, PER, 16, rest), BF16),
             pltpu.VMEM((16, rest), F32),
             pltpu.VMEM((NZ, 16, rest), BF16),
             pltpu.VMEM((2, 2, 3, 4, 16, NARROW), BF16),
@@ -441,7 +442,7 @@
             pltpu.VMEM((16, width), F32),
             dma,
             dma((PARTS, 4)), dma((PARTS, 4)), dma((PARTS, 4)), dma((PARTS, 4)),
-            dma((PARTS, 3)), dma((NZ,)),
+            dma((PARTS, PER)), dma((NZ,)),
             dma((SPANS,)), dma, dma((NS,)), dma((NS,)),
             dma((BLOCKS, SPANS)), dma, dma((16,)), dma,
             pltpu.SemaphoreType.REGULAR((2, 2)),

time: 59.4 us -> 59.2 us (level)
  no operation moved by 1% of the time
where the time goes in v5:
time: 59.2 us; the launch traced here: 59 us
  Pallas kernels  57 us (96%)
  local copies, waits for them, and re-layouts  2.02 us (3%)
    pallas_call x1, Pallas kernels, body(): pl.pallas_call(kernel, out_shape=jax.ShapeDtypeStruct((16, width), F32),...  57 us
    unnamed x3, local copies, waits for them, and re-layouts  2.02 us

profile of v5, /device:TPU:8, one launch (start us, length us, event | category | flops | bytes accessed | tf_op | source)
XLA Modules:
  0.0 59.0 jit_solution(12486012088502138407)
XLA Ops:
  0.0 0.0 copy-start
  0.0 1.4 %copy-done = bf16[1,1,1536,512]{3,2,1,0:T(8,128)(2,1)S(1)} copy-done((bf16[1,1,1536,512]{3,2,1,0:T(8,128)(2,1)S(1)}, bf16[1,1,1536,512]{3,2,1,0:T(8,128)(2,1)}, u32[]{:S(2)}) %copy-start) | copy-done | bytes 1572888
  1.4 57.0 %shard_map.17 = f32[16,512]{1,0:T(8,128)S(1)} custom-call(bf16[8,6,2,16,512]{4,3,2,1,0:T(8,128)(2,1)S(1)} %bitcast.2), custom_call_target="tpu_custom_call" | custom-call | tf_op jit(solution)/shard_map/pallas_call | solution.py:415
  58.4 0.6 %copy.3 = f32[1,16,512]{2,1,0:T(8,128)} copy(f32[1,16,512]{2,1,0:T(8,128)S(1)} %bitcast.3) | data formatting | bytes 65536
Async XLA Ops:
  0.0 1.4 %copy-start = (bf16[1,1,1536,512]{3,2,1,0:T(8,128)(2,1)S(1)}, bf16[1,1,1536,512]{3,2,1,0:T(8,128)(2,1)}, u32[]{:S(2)}) copy-start(bf16[1,1,1536,512]{3,2,1,0:T(8,128)(2,1)} %param.1) | copy-start | bytes 4718596
